TPU v7x, 32 devices: a whole 2x2x4 slice. The times are simulated.
32 devices in a mesh: field: 16 (over z, y, x), batch: 2 (over core).
Axes of the slice: x: 2, y: 2, z: 4, core: 2. Of those that a mesh axis runs over, the one named last changes fastest.
Arguments:
- pooled: bfloat16 [1024, 16, 256], P('batch', 'field'), may hold values from -6 to 6
- counts: int32 [1024, 16], P('batch', 'field'), may hold values from 1 to 16
- w_pairs: bfloat16 [16, 120, 1024], P('field', None, 'batch'), may hold values from -0.125 to 0.125
- bias_terms: bfloat16 [1024], P('batch'), may hold values from -4 to 4
- grad_act: bfloat16 [1024, 1024], P('batch'), may hold values from -6 to 6
Outputs:
- entry_grad: bfloat16 [1024, 16, 256], P('batch', 'field')
- weight_grad: float32 [16, 120, 1024], P('field', None, 'batch')
All inputs are finite; a program needn't handle non-finite values.
Results may differ from a plain program's by a relative error of at most 0.014.
Values may be sent and summed in bfloat16 or wider, within the bound.
A program may use at most 64 MiB of HBM per device.

v0:
```python
import jax
import jax.numpy as jnp
from jax import lax
from jax.sharding import PartitionSpec as P


def body(pooled, counts, w_pairs, bias_terms, grad_act):
    sample_rows = pooled.shape[0]
    fields = lax.axis_size("field")
    depth = pooled.shape[2] // fields
    half_depth = depth // 2
    my_field = lax.axis_index("field")
    embedded = pooled.reshape(sample_rows, fields, depth)
    partner = jnp.arange(fields, dtype=jnp.int32)[None, :, None]
    upper_half = partner < my_field
    mine = jnp.where(upper_half, embedded[..., half_depth:], embedded[..., :half_depth])
    outbound = jnp.where(upper_half, embedded[..., :half_depth], embedded[..., half_depth:])
    received = lax.all_to_all(
        outbound.reshape(sample_rows, fields * half_depth),
        "field",
        split_axis=1,
        concat_axis=1,
        tiled=True,
    )
    received = received.reshape(sample_rows, fields, half_depth).astype(jnp.float32)
    product_all = (mine.astype(jnp.float32) * received).astype(jnp.bfloat16)
    slot_index = jnp.arange(fields - 1, dtype=jnp.int32)[None, :, None]
    pair_rows = jnp.where(slot_index >= my_field, product_all[:, 1:], product_all[:, :-1])
    pair_rows = pair_rows.reshape(sample_rows, (fields - 1) * half_depth)
    weight_cols, bias_wide = (
        lax.all_gather(w_pairs[0], "batch", axis=1, tiled=True),
        lax.all_gather(bias_terms, "batch", axis=0, tiled=True),
    )
    bias_float = bias_wide.astype(jnp.float32)
    partial_hidden = jnp.dot(pair_rows, weight_cols, preferred_element_type=jnp.float32)
    hidden = lax.psum(partial_hidden, "field")
    preact = hidden + bias_float
    gate_value = jax.nn.sigmoid(preact)
    slope_act = (
        grad_act.astype(jnp.float32) * gate_value * (1.0 + preact * (1.0 - gate_value))
    ).astype(jnp.bfloat16)
    pair_grad = lax.dot_general(
        slope_act, weight_cols, (((1,), (1,)), ((), ())), preferred_element_type=jnp.float32
    )
    pair_grad = pair_grad.reshape(sample_rows, fields - 1, half_depth)
    weight_term = lax.dot_general(
        pair_rows, slope_act, (((0,), (0,)), ((), ())), preferred_element_type=jnp.float32
    )
    weight_grad = lax.psum_scatter(
        weight_term.astype(jnp.bfloat16), "batch", scatter_dimension=1, tiled=True
    ).astype(jnp.float32)
    zero_slot = jnp.zeros((sample_rows, 1, half_depth), jnp.float32)
    below_slots = jnp.concatenate([pair_grad, zero_slot], 1)
    above_slots = jnp.concatenate([zero_slot, pair_grad], 1)
    dense_grad = jnp.where(
        partner < my_field, below_slots, jnp.where(partner > my_field, above_slots, 0.0)
    )
    local_part = dense_grad * received
    outgoing = (
        (dense_grad * mine.astype(jnp.float32))
        .astype(jnp.bfloat16)
        .reshape(sample_rows, fields * half_depth)
    )
    returned = (
        lax.all_to_all(outgoing, "field", split_axis=1, concat_axis=1, tiled=True)
        .reshape(sample_rows, fields, half_depth)
        .astype(jnp.float32)
    )
    full_grad = jnp.where(
        upper_half,
        jnp.concatenate([returned, local_part], -1),
        jnp.concatenate([local_part, returned], -1),
    )
    full_grad = full_grad / jnp.sqrt(counts.astype(jnp.float32))[:, :, None]
    return (
        full_grad.reshape(sample_rows, 1, fields * depth).astype(jnp.bfloat16),
        weight_grad[None],
    )


def solution(mesh):
    in_specs = (
        P("batch", "field", None),
        P("batch", "field"),
        P("field", None, "batch"),
        P("batch"),
        P("batch", None),
    )
    out_specs = (P("batch", "field", None), P("field", None, "batch"))
    return jax.shard_map(body, mesh=mesh, in_specs=in_specs, out_specs=out_specs, check_vma=False)
```

profile of v0, /device:TPU:0, one launch (start us, length us, event | category | flops | bytes accessed | tf_op | source)
XLA Modules:
  0.0 180.8 jit_solution(18044973064926914177)
XLA Ops:
  7.2 1.1 copy.13
  8.3 0.7 broadcast_select_fusion
  9.0 8.3 %all-to-all-start = ((bf16[512,16,8]{0,2,1:T(8,128)(2,1)}), bf16[512,16,8]{0,2,1:T(8,128)(2,1)S(1)}, u32[]{:S(2)}, u32[]{:S(2)}) async-start(bf16[512,16,8]{0,2,1:T(8,128)(2,1)} %broadcast_select_fusion), calls=%async_computation | async-start | bytes 262144 | tf_op jit(solution)/shard_map/all_to_all | solution.py:18
  17.3 0.0 all-reduce.4.cloned.1.call-start
  17.4 2.3 %all-gather = bf16[1,120,1024]{2,1,0:T(8,128)(2,1)S(1)} all-gather(bf16[1,120,512]{2,1,0:T(8,128)(2,1)} %param.7), channel_id=2, replica_groups=mesh['field'=16,'batch'=2] {'batch'}, dimensions={2}, use_global_device_ids=true | all-gather | bytes 368640 | tf_op jit(solution)/shard_map/all_gather | solution.py:31
  19.7 5.4 %all-to-all-done = bf16[512,16,8]{0,2,1:T(8,128)(2,1)S(1)} async-done(((bf16[512,16,8]{0,2,1:T(8,128)(2,1)}), bf16[512,16,8]{0,2,1:T(8,128)(2,1)S(1)}, u32[]{:S(2)}, u32[]{:S(2)}) %all-to-all-start) | async-done | bytes 131104 | tf_op jit(solution)/shard_map/all_to_all | solution.py:18
  25.1 0.1 fusion.3
  25.3 1.9 %fusion.5 = f32[512,1024]{1,0:T(8,128)} fusion(bf16[1,120,1024]{2,1,0:T(8,128)(2,1)S(1)} %all-gather, bf16[512,16,8]{0,2,1:T(8,128)(2,1)S(1)} %fusion.3, pred[15]{0:T(512)(128)(4,1)S(1)} %iota_compare_fusion.1), kind=kOutput, calls=%fused_computation.15 | convolution fusion | flops 125890560 | bytes 2589184 | tf_op jit(solution)/shard_map/dot_general | solution.py:35
  27.2 1.8 all-gather.1
  29.0 121.9 %all-reduce.4.cloned.1.call-done = f32[512,1024]{1,0:T(8,128)} async-done(((f32[512,1024]{1,0:T(8,128)}), f32[512,1024]{1,0:T(8,128)}) %all-reduce.4.cloned.1.call-update) | async-done | bytes 2097168 | tf_op jit(solution)/shard_map/psum | solution.py:36
  150.9 2.4 %multiply_convert_fusion = bf16[512,1024]{1,0:T(8,128)(2,1)S(1)} fusion(f32[512,1024]{1,0:T(8,128)} %all-reduce.4.cloned.1.call-done, bf16[512,1024]{1,0:T(8,128)(2,1)S(1)} %copy-done, f32[1024]{0:T(1024)S(1)} %bitcast.34), kind=kLoop, calls=%fused_computation | loop fusion | flops 5767168 | bytes 4198400 | tf_op jit(solution)/shard_map/convert_element_type | solution.py:41
  153.3 0.5 convolution_bitcast_fusion
  153.8 0.8 convert_multiply_fusion
  154.6 5.0 %all-to-all-start.1 = ((bf16[512,16,8]{0,2,1:T(8,128)(2,1)}), bf16[512,16,8]{0,2,1:T(8,128)(2,1)S(1)}, u32[]{:S(2)}, u32[]{:S(2)}) async-start(bf16[512,16,8]{0,2,1:T(8,128)(2,1)} %get-tuple-element.9), calls=%async_computation.1 | async-start | bytes 262144 | tf_op jit(solution)/shard_map/all_to_all | solution.py:65
  159.6 0.0 reduce-scatter.2.cloned.1.call-start
  159.7 1.0 convolution_convert_fusion
  160.8 0.1 broadcast_in_dim.60
  160.8 0.1 broadcast_in_dim.61
  160.9 6.5 %all-to-all-done.1 = bf16[512,16,8]{0,2,1:T(8,128)(2,1)S(1)} async-done(((bf16[512,16,8]{0,2,1:T(8,128)(2,1)}), bf16[512,16,8]{0,2,1:T(8,128)(2,1)S(1)}, u32[]{:S(2)}, u32[]{:S(2)}) %all-to-all-start.1) | async-done | bytes 131104 | tf_op jit(solution)/shard_map/all_to_all | solution.py:65
  167.4 0.1 pad_maximum_fusion
  167.6 0.1 fusion.1
  167.7 0.8 copy.14
  168.5 3.7 %reduce-scatter.2.cloned.1.call-done = bf16[120,512]{1,0:T(8,128)(2,1)} async-done(((bf16[120,1024]{1,0:T(8,128)(2,1)}), bf16[120,512]{1,0:T(8,128)(2,1)}) %reduce-scatter.2.cloned.1.call-update) | async-done | bytes 122896 | tf_op jit(solution)/shard_map/reduce_scatter | solution.py:49
  172.3 1.6 bitcast_convert_fusion
  (15 shorter events, 0.1 us)
Async XLA Ops:
  9.0 16.1 %all-to-all-start = ((bf16[512,16,8]{0,2,1:T(8,128)(2,1)}), bf16[512,16,8]{0,2,1:T(8,128)(2,1)S(1)}, u32[]{:S(2)}, u32[]{:S(2)}) async-start(bf16[512,16,8]{0,2,1:T(8,128)(2,1)} %broadcast_select_fusion), calls=%async_computation | async-start | bytes 262144 | tf_op jit(solution)/shard_map/all_to_all | solution.py:18
  17.3 133.6 %all-reduce.4.cloned.1.call-start = ((), (), s32[]{:S(2)}) async-start(), calls=%async_computation.3 | async-start | bytes 4194304 | tf_op jit(solution)/shard_map/psum | solution.py:36
  25.3 1.9 %copy-start.2 = (bf16[512]{0:T(512)(128)(2,1)S(1)}, bf16[512]{0:T(512)(128)(2,1)}, u32[]{:S(2)}) copy-start(bf16[512]{0:T(512)(128)(2,1)} %param.8) | copy-start | bytes 3076
  25.3 125.6 %copy-start = (bf16[512,1024]{1,0:T(8,128)(2,1)S(1)}, bf16[512,1024]{1,0:T(8,128)(2,1)}, u32[]{:S(2)}) copy-start(bf16[512,1024]{1,0:T(8,128)(2,1)} %param.9) | copy-start | bytes 3145732
  153.3 7.4 %copy-start.1 = (s32[512,1]{0,1:T(1,128)S(1)}, s32[512,1]{0,1:T(1,128)}, u32[]{:S(2)}) copy-start(s32[512,1]{0,1:T(1,128)} %param.6) | copy-start | bytes 6148
  154.6 12.8 %all-to-all-start.1 = ((bf16[512,16,8]{0,2,1:T(8,128)(2,1)}), bf16[512,16,8]{0,2,1:T(8,128)(2,1)S(1)}, u32[]{:S(2)}, u32[]{:S(2)}) async-start(bf16[512,16,8]{0,2,1:T(8,128)(2,1)} %get-tuple-element.9), calls=%async_computation.1 | async-start | bytes 262144 | tf_op jit(solution)/shard_map/all_to_all | solution.py:65
  159.6 12.7 %reduce-scatter.2.cloned.1.call-start = ((), (), s32[]{:S(2)}) async-start(), calls=%async_computation.4 | async-start | bytes 368640 | tf_op jit(solution)/shard_map/reduce_scatter | solution.py:49
Sparse Core Ops, SparseCore 0:
  27.3 123.5 all-reduce.3
  163.4 8.8 reduce-scatter.1
where the time goes:
time: 181 us
  waiting for transfers between devices  138 us (76%)
  between operations  14.2 us (8%)
  starting transfers between devices  13.4 us (7%)
  other arithmetic  6 us (3%)
  blocking collectives  4.08 us (2%)
  matrix products  3.37 us (2%)
  local copies, waits for them, and re-layouts  2.12 us (1%)
    psum x1, waiting for transfers between devices, body(): hidden = lax.psum(partial_hidden, 'field')  122 us
    all_to_all x1, starting transfers between devices, body(): lax.all_to_all(outbound.reshape(sample_rows, fields * half_depth), 'field...  8.31 us
    all_to_all x1, waiting for transfers between devices, body(): lax.all_to_all(outgoing, 'field', split_axis=1, concat_axis=1, tiled=True)  6.49 us
    all_to_all x1, waiting for transfers between devices, body(): lax.all_to_all(outbound.reshape(sample_rows, fields * half_depth), 'field...  5.44 us
    all_to_all x1, starting transfers between devices, body(): lax.all_to_all(outgoing, 'field', split_axis=1, concat_axis=1, tiled=True)  4.97 us
    reduce_scatter x1, waiting for transfers between devices, body(): lax.psum_scatter(weight_term.astype(jnp.bfloat16), 'batch', scatter_dimen...  3.75 us
  transfers between devices with their start and end apart: 4, of which 4 were waited for; matrix products, arithmetic and copies ran while one was open for 1% of the time, Pallas kernels for 0%

commit v1 on v0

v1 whole, which is shorter than its diff:
```python
import functools

import jax
import jax.numpy as jnp
from jax import lax
from jax.experimental import pallas as pl
from jax.experimental.pallas import tpu as pltpu
from jax.sharding import PartitionSpec as P

MESH = pl.DeviceIdType.MESH
F32 = jnp.float32
BF16 = jnp.bfloat16


def fold_rows(x, parts):
    if parts == 1:
        return x
    width = x.shape[2] // parts
    return jnp.concatenate([x[:, :, p * width:(p + 1) * width] for p in range(parts)], axis=1)


def unfold_rows(x, parts):
    if parts == 1:
        return x
    height = x.shape[1] // parts
    return jnp.concatenate([x[:, p * height:(p + 1) * height, :] for p in range(parts)], axis=2)


def kernel(fields, shards, fold, e_ref, cnt_ref, w_ref, b_ref, g_hbm, eg_ref, wg_ref,
           out1, in1, mine_v, rec_v, w_all, pairs_t, pairs, send2, in2, acc, g_blk,
           slope_all, out3, in3, wg_out, wg_in, wg_acc,
           s1, r1, sw, rw, s2, r2, sg, rg, s3, r3, sx, rx, sl):
    f = lax.axis_index("field")
    c = lax.axis_index("batch")
    samples = e_ref.shape[0]
    hid = g_hbm.shape[2]
    rows = samples // fields
    part = w_ref.shape[1]
    half = 8
    pair_count = fields * half

    barrier = pltpu.get_barrier_semaphore()

    def greet(d, carry):
        pl.semaphore_signal(barrier, inc=1, device_id={"field": lax.rem(f + d, fields)}, device_id_type=MESH)
        return carry

    def greet_batch(d, carry):
        pl.semaphore_signal(barrier, inc=1, device_id={"batch": lax.rem(c + d, shards)}, device_id_type=MESH)
        return carry

    lax.fori_loop(1, fields, greet, 0)
    lax.fori_loop(1, shards, greet_batch, 0)

    g_copy = pltpu.make_async_copy(g_hbm.at[f], g_blk, sl)
    g_copy.start()

    e_t = e_ref[...].astype(F32).T.reshape(fields, 2 * half, samples)
    block = lax.broadcasted_iota(jnp.int32, (fields, half, samples), 0)
    below = block < f
    low, high = e_t[:, :half, :], e_t[:, half:, :]
    mine_v[...] = jnp.where(below, high, low)
    out1[...] = fold_rows(jnp.where(below, low, high), 2).astype(BF16)
    blank = jnp.zeros((1,) + in1.shape[1:], BF16)
    in1[pl.ds(f, 1)] = blank
    in3[pl.ds(f, 1)] = blank

    w_slots = w_ref[...].astype(F32).reshape(fields - 1, half, part)
    gap = jnp.zeros((1, half, part), F32)
    w_block = lax.broadcasted_iota(jnp.int32, (fields, half, part), 0)
    w_wide = jnp.where(
        w_block < f,
        jnp.concatenate([w_slots, gap], 0),
        jnp.where(w_block > f, jnp.concatenate([gap, w_slots], 0), 0.0),
    )
    bias = jnp.broadcast_to(b_ref[...].astype(F32), (16, part))
    w_all[c] = jnp.concatenate([w_wide.reshape(pair_count, part), bias], 0).astype(BF16)

    pl.semaphore_wait(barrier, fields - 1 + shards - 1)

    def copy1(d):
        to = lax.rem(f + d, fields)
        return pltpu.make_async_remote_copy(
            out1.at[to], in1.at[f], s1.at[d], r1.at[d], device_id={"field": to}, device_id_type=MESH)

    def copyw(d):
        return pltpu.make_async_remote_copy(
            w_all.at[c], w_all.at[c], sw.at[d], rw.at[d],
            device_id={"batch": lax.rem(c + d, shards)}, device_id_type=MESH)

    def copy2(d):
        to = lax.rem(f + d, fields)
        return pltpu.make_async_remote_copy(
            send2.at[to], in2.at[f], s2.at[d], r2.at[d], device_id={"field": to}, device_id_type=MESH)

    def copyg(d):
        to = lax.rem(f + d, fields)
        return pltpu.make_async_remote_copy(
            slope_all.at[f], slope_all.at[f], sg.at[d], rg.at[d], device_id={"field": to}, device_id_type=MESH)

    def copy3(d):
        to = lax.rem(f + d, fields)
        return pltpu.make_async_remote_copy(
            out3.at[to], in3.at[f], s3.at[d], r3.at[d], device_id={"field": to}, device_id_type=MESH)

    def copyx(d):
        to = lax.rem(c + d, shards)
        return pltpu.make_async_remote_copy(
            wg_out.at[to], wg_in.at[c], sx.at[d], rx.at[d], device_id={"batch": to}, device_id_type=MESH)

    def each(count, copy, action):
        def step(d, carry):
            action(copy(d))
            return carry
        lax.fori_loop(1, count, step, 0)

    def wait_in(copy):
        copy.wait_recv()

    def wait_out(copy):
        copy.wait_send()

    def go(copy):
        copy.start()

    each(fields, copy1, go)
    each(shards, copyw, go)
    each(fields, copy1, wait_in)
    received = unfold_rows(in1[...].astype(F32), 2)
    rec_v[...] = received
    product = (mine_v[...] * received).reshape(pair_count, samples)
    pairs_t[...] = product.astype(BF16)
    pairs[...] = product.T.astype(BF16)
    each(shards, copyw, wait_in)

    weights = jnp.concatenate([w_all[s, :pair_count, :] for s in range(shards)], axis=1)
    chunks = 4
    per = fields // chunks

    def hidden_chunk(q, carry):
        lhs = pairs[pl.ds(pl.multiple_of(q * (per * rows), per * rows), per * rows), :]
        part_hidden = jnp.dot(lhs, weights, preferred_element_type=F32).reshape(per, rows, hid)
        send2[pl.ds(q * per, per)] = fold_rows(part_hidden, fold).astype(BF16)
        return carry

    lax.fori_loop(0, chunks, hidden_chunk, 0)
    each(fields, copy2, go)
    in2[f] = send2[f]
    each(fields, copy2, wait_in)

    acc[...] = in2[0].astype(F32)

    def add(j, carry):
        acc[...] += in2[j].astype(F32)
        return carry

    lax.fori_loop(1, fields, add, 0)
    g_copy.wait()
    bias_all = jnp.concatenate([w_all[s, pair_count:, :][:1].astype(F32) for s in range(shards)], axis=1)
    hidden = unfold_rows(acc[...][None], fold)[0] + bias_all
    gate = jax.nn.sigmoid(hidden)
    slope = g_blk[...].astype(F32) * gate * (1.0 + hidden * (1.0 - gate))
    slope_all[f] = fold_rows(slope[None], fold)[0].astype(BF16)
    each(fields, copyg, go)
    each(fields, copyg, wait_in)

    if fold == 1:
        slope_full = slope_all[...].reshape(samples, hid)
    else:
        slope_full = unfold_rows(slope_all[...].astype(F32), fold).reshape(samples, hid).astype(BF16)
    grad_t = lax.dot_general(weights, slope_full, (((1,), (1,)), ((), ())), preferred_element_type=F32)
    grad_t = grad_t.reshape(fields, half, samples)
    out3[...] = fold_rows(grad_t * mine_v[...], 2).astype(BF16)
    each(fields, copy3, go)
    rec_v[...] = grad_t * rec_v[...]

    term = jnp.dot(pairs_t[...], slope_full, preferred_element_type=F32)
    for s in range(shards):
        wg_acc[s] = term[:, s * part:(s + 1) * part]
    wg_out[...] = wg_acc[...].astype(BF16)
    each(shards, copyx, go)

    scale = 1.0 / jnp.sqrt(cnt_ref[...].astype(F32))
    each(fields, copy3, wait_in)
    back = unfold_rows(in3[...].astype(F32), 2) * scale[None]
    local = rec_v[...] * scale[None]
    full = jnp.concatenate([jnp.where(below, back, local), jnp.where(below, local, back)], axis=1)
    eg_ref[...] = full.reshape(fields * 2 * half, samples).T.astype(BF16)

    each(shards, copyx, wait_in)
    wg_out_sum = wg_acc[c]

    def add_wg(d, total):
        return total + wg_in[lax.rem(c + d, shards)].astype(F32)

    for d in range(1, shards):
        wg_out_sum = add_wg(d, wg_out_sum)
    wg3 = wg_out_sum.reshape(fields, half, part)
    slot = lax.broadcasted_iota(jnp.int32, (fields - 1, half, part), 0)
    wg_ref[...] = jnp.where(slot < f, wg3[:-1], wg3[1:]).reshape(pair_count - half, part)

    for count, copy in ((fields, copy1), (shards, copyw), (fields, copy2), (fields, copyg),
                        (fields, copy3), (shards, copyx)):
        each(count, copy, wait_out)


def body(pooled, counts, w_pairs, bias_terms, grad_act):
    fields = lax.axis_size("field")
    shards = lax.axis_size("batch")
    samples = pooled.shape[0]
    width = pooled.shape[2]
    part = w_pairs.shape[2]
    hid = grad_act.shape[1]
    half = width // fields // 2
    rows = samples // fields
    fold = max(1, 16 // rows)
    pair_count = fields * half
    packed = (fields, 2 * half, samples // 2)
    block = (fields, rows * fold, hid // fold)
    vmem = pl.BlockSpec(memory_space=pltpu.VMEM)
    dma = pltpu.SemaphoreType.DMA
    entry, weight = pl.pallas_call(
        functools.partial(kernel, fields, shards, fold),
        out_shape=(
            jax.ShapeDtypeStruct((samples, width), BF16),
            jax.ShapeDtypeStruct((pair_count - half, part), F32),
        ),
        in_specs=[vmem, vmem, vmem, vmem, pl.BlockSpec(memory_space=pl.ANY)],
        out_specs=(vmem, vmem),
        scratch_shapes=[
            pltpu.VMEM(packed, BF16),
            pltpu.VMEM(packed, BF16),
            pltpu.VMEM((fields, half, samples), F32),
            pltpu.VMEM((fields, half, samples), F32),
            pltpu.VMEM((shards, pair_count + 16, part), BF16),
            pltpu.VMEM((pair_count, samples), BF16),
            pltpu.VMEM((samples, pair_count), BF16),
            pltpu.VMEM(block, BF16),
            pltpu.VMEM(block, BF16),
            pltpu.VMEM(block[1:], F32),
            pltpu.VMEM((rows, hid), BF16),
            pltpu.VMEM(block, BF16),
            pltpu.VMEM(packed, BF16),
            pltpu.VMEM(packed, BF16),
            pltpu.VMEM((shards, pair_count, part), BF16),
            pltpu.VMEM((shards, pair_count, part), BF16),
            pltpu.VMEM((shards, pair_count, part), F32),
            dma((fields,)), dma((fields,)), dma((shards,)), dma((shards,)),
            dma((fields,)), dma((fields,)), dma((fields,)), dma((fields,)),
            dma((fields,)), dma((fields,)), dma((shards,)), dma((shards,)), dma,
        ],
        compiler_params=pltpu.CompilerParams(
            collective_id=0, has_side_effects=True, vmem_limit_bytes=48 * 1024 * 1024),
    )(
        pooled.reshape(samples, width),
        counts.reshape(1, samples),
        w_pairs[0],
        bias_terms.reshape(1, part),
        grad_act.reshape(fields, rows, hid),
    )
    return entry.reshape(samples, 1, width), weight[None]


def solution(mesh):
    in_specs = (
        P("batch", "field", None),
        P("batch", "field"),
        P("field", None, "batch"),
        P("batch"),
        P("batch", None),
    )
    out_specs = (P("batch", "field", None), P("field", None, "batch"))
    return jax.shard_map(body, mesh=mesh, in_specs=in_specs, out_specs=out_specs, check_vma=False)
```

time: 181 us -> 73.9 us (0.41)
  waiting for transfers between devices: 138 us -> 0 us
  Pallas kernels: 0 us -> 67.8 us
  between operations: 14.2 us -> 0.66 us
  starting transfers between devices: 13.4 us -> 0 us
  other arithmetic: 6 us -> 0 us
  blocking collectives: 4.08 us -> 0 us
  matrix products: 3.37 us -> 0 us
  local copies, waits for them, and re-layouts: 2.12 us -> 5.15 us
    psum x1 -> x0, waiting for transfers between devices: 122 us -> none  [body(): hidden = lax.psum(partial_hidden, 'field')]
    pallas_call x0 -> x1, Pallas kernels: none -> 67.8 us  [body(): pl.pallas_call(functools.partial(kernel, fields, shards, fold), out_shape...]
    all_to_all x2 -> x0, starting transfers between devices: 13.3 us -> none  [the longest x1 8.31 us: body(): lax.all_to_all(outbound.reshape(sample_rows, fields * half_depth), 'field...]
    all_to_all x2 -> x0, waiting for transfers between devices: 11.9 us -> none  [the longest x1 6.49 us: body(): lax.all_to_all(outgoing, 'field', split_axis=1, concat_axis=1, tiled=True)]
    all_gather x2 -> x0, blocking collectives: 4.08 us -> none  [the longest x1 2.3 us: body(): lax.all_gather(w_pairs[0], 'batch', axis=1, tiled=True)]
    reduce_scatter x1 -> x0, waiting for transfers between devices: 3.75 us -> none  [body(): lax.psum_scatter(weight_term.astype(jnp.bfloat16), 'batch', scatter_dimen...]
    dot_general x3 -> x0, matrix products: 3.37 us -> none  [the longest x1 1.85 us: body(): jnp.dot(pair_rows, weight_cols, preferred_element_type=jnp.float32)]
    unnamed x9 -> x12, local copies, waits for them, and re-layouts: 1.96 us -> 5.15 us
  transfers between devices with their start and end apart: 4 -> 0, of which waited for: 4 -> 0; matrix products, arithmetic and copies ran while one was open for 1% -> 0% of each run, Pallas kernels for 0% -> 0%
where the time goes in v1:
time: 73.9 us; the launch traced here: 73.6 us
  Pallas kernels  67.8 us (92%)
  local copies, waits for them, and re-layouts  5.15 us (7%)
    pallas_call x1, Pallas kernels, body(): pl.pallas_call(functools.partial(kernel, fields, shards, fold), out_shape...  67.8 us
    unnamed x12, local copies, waits for them, and re-layouts  5.15 us

profile of v1, /device:TPU:0, one launch (start us, length us, event | category | flops | bytes accessed | tf_op | source)
XLA Modules:
  0.0 73.6 jit_solution(8033817185477245893)
XLA Ops:
  0.6 0.0 copy-start.4
  0.6 0.0 copy-start.3
  0.6 0.7 copy-done.4
  1.3 0.0 copy-done.3
  1.3 0.0 copy-start
  1.3 1.2 %copy-done = bf16[512,1024]{1,0:T(8,128)(2,1)S(1)} copy-done((bf16[512,1024]{1,0:T(8,128)(2,1)S(1)}, bf16[512,1024]{1,0:T(8,128)(2,1)}, u32[]{:S(2)}) %copy-start) | copy-done | bytes 1048600
  2.6 0.0 copy-start.1
  2.6 0.9 %copy-done.1 = bf16[512,1,256]{2,0,1:T(8,128)(2,1)S(1)} copy-done((bf16[512,1,256]{2,0,1:T(8,128)(2,1)S(1)}, bf16[512,1,256]{2,0,1:T(8,128)(2,1)}, u32[]{:S(2)}) %copy-start.1) | copy-done | bytes 262168
  3.5 0.0 copy-start.2
  3.5 0.9 %copy-done.2 = bf16[1,120,512]{2,1,0:T(8,128)(2,1)S(1)} copy-done((bf16[1,120,512]{2,1,0:T(8,128)(2,1)S(1)}, bf16[1,120,512]{2,1,0:T(8,128)(2,1)}, u32[]{:S(2)}) %copy-start.2) | copy-done | bytes 122904
  4.4 67.8 %shard_map.68 = (bf16[512,256]{1,0:T(8,128)(2,1)S(1)}, f32[120,512]{1,0:T(8,128)S(1)}) custom-call(bf16[512,256]{1,0:T(8,128)(2,1)S(1)} %bitcast.8, s32[1,512]{1,0:T(1,128)S(1)} %bitcast.11, bf16[120,512]{1,0:T(8,128)(2,1)S(1)} %bitcast.10, bf16[1,512]{1,0:T(2,128)(2,1)S(1)} %reshape.21.b_ref, bf16[16,32,1024]{2,1,0:T(8,128)(2,1)S(1)} %bitcast.6), custom_call_target="tpu_custom_call" | custom-call | tf_op jit(solution)/shard_map/pallas_call | solution.py:222
  72.2 0.7 copy.9
  72.9 0.7 copy.10
  (1 shorter events, 0.0 us)
Async XLA Ops:
  0.6 0.7 copy-start.4
  0.6 0.7 copy-start.3
  1.3 1.2 %copy-start = (bf16[512,1024]{1,0:T(8,128)(2,1)S(1)}, bf16[512,1024]{1,0:T(8,128)(2,1)}, u32[]{:S(2)}) copy-start(bf16[512,1024]{1,0:T(8,128)(2,1)} %param.9) | copy-start | bytes 3145732
  2.6 0.9 %copy-start.1 = (bf16[512,1,256]{2,0,1:T(8,128)(2,1)S(1)}, bf16[512,1,256]{2,0,1:T(8,128)(2,1)}, u32[]{:S(2)}) copy-start(bf16[512,1,256]{2,0,1:T(8,128)(2,1)} %param.5) | copy-start | bytes 786436
  3.5 0.9 %copy-start.2 = (bf16[1,120,512]{2,1,0:T(8,128)(2,1)S(1)}, bf16[1,120,512]{2,1,0:T(8,128)(2,1)}, u32[]{:S(2)}) copy-start(bf16[1,120,512]{2,1,0:T(8,128)(2,1)} %param.7) | copy-start | bytes 368644

commit v2 on v1

v2 whole, which is shorter than its diff:
```python
import functools

import jax
import jax.numpy as jnp
from jax import lax
from jax.experimental import pallas as pl
from jax.experimental.pallas import tpu as pltpu
from jax.sharding import PartitionSpec as P

MESH = pl.DeviceIdType.MESH
F32 = jnp.float32
BF16 = jnp.bfloat16


def fold_rows(x, parts):
    if parts == 1:
        return x
    width = x.shape[2] // parts
    return jnp.concatenate([x[:, :, p * width:(p + 1) * width] for p in range(parts)], axis=1)


def unfold_rows(x, parts):
    if parts == 1:
        return x
    height = x.shape[1] // parts
    return jnp.concatenate([x[:, p * height:(p + 1) * height, :] for p in range(parts)], axis=2)


def kernel(fields, shards, fold, e_hbm, cnt_ref, w_hbm, b_ref, g_hbm, eg_ref, wg_ref,
           e_ref, w_ref, out1, in1, mine_v, rec_v, w_all, pairs_t, pairs, g_blk,
           keep1, o1, i1, keep2, o2, i2, o3, i3, acc,
           slope_all, out3, in3, wg_out, wg_in, wg_acc,
           s1, r1, sw, rw, s3, r3, sx, rx,
           sa1, ra1, sb1, rb1, sa2, ra2, sb2, rb2, sz3, rz3,
           szg, rzg, sxg, rxg, syg, ryg, sxd, rxd, syd, ryd, sl):
    f = lax.axis_index("field")
    c = lax.axis_index("batch")
    samples = e_ref.shape[0]
    hid = g_hbm.shape[2]
    rows = samples // fields
    part = w_ref.shape[1]
    half = 8
    pair_count = fields * half
    depth = fields // 4
    x = lax.rem(f, 2)
    y = lax.rem(f // 2, 2)
    z = f // 4
    plane = lax.rem(f, 4)
    x_peer = f + 1 - 2 * x
    y_peer = f + 2 - 4 * y

    e_copy = pltpu.make_async_copy(e_hbm, e_ref, sl.at[0])
    w_copy = pltpu.make_async_copy(w_hbm, w_ref, sl.at[1])
    g_copy = pltpu.make_async_copy(g_hbm.at[f], g_blk, sl.at[2])
    e_copy.start()
    w_copy.start()
    g_copy.start()

    barrier = pltpu.get_barrier_semaphore()

    def greet(d, carry):
        pl.semaphore_signal(barrier, inc=1, device_id={"field": lax.rem(f + d, fields)}, device_id_type=MESH)
        return carry

    def greet_batch(d, carry):
        pl.semaphore_signal(barrier, inc=1, device_id={"batch": lax.rem(c + d, shards)}, device_id_type=MESH)
        return carry

    lax.fori_loop(1, fields, greet, 0)
    lax.fori_loop(1, shards, greet_batch, 0)

    e_copy.wait()
    e_t = e_ref[...].astype(F32).T.reshape(fields, 2 * half, samples)
    block = lax.broadcasted_iota(jnp.int32, (fields, half, samples), 0)
    below = block < f
    low, high = e_t[:, :half, :], e_t[:, half:, :]
    mine_v[...] = jnp.where(below, high, low)
    out1[...] = fold_rows(jnp.where(below, low, high), 2).astype(BF16)
    blank = jnp.zeros((1,) + in1.shape[1:], BF16)
    in1[pl.ds(f, 1)] = blank
    in3[pl.ds(f, 1)] = blank

    def copy1(d):
        to = lax.rem(f + d, fields)
        return pltpu.make_async_remote_copy(
            out1.at[to], in1.at[f], s1.at[d], r1.at[d], device_id={"field": to}, device_id_type=MESH)

    def copyw(d):
        return pltpu.make_async_remote_copy(
            w_all.at[c], w_all.at[c], sw.at[d], rw.at[d],
            device_id={"batch": lax.rem(c + d, shards)}, device_id_type=MESH)

    def send(src, dst, s, r, to):
        return pltpu.make_async_remote_copy(
            src, dst, s, r, device_id={"field": to}, device_id_type=MESH)

    def copy_a1(i):
        return send(o1.at[i, 0], i1.at[i, 0], sa1.at[i], ra1.at[i], x_peer)

    def copy_b1(i):
        return send(o1.at[i, 1], i1.at[i, 1], sb1.at[i], rb1.at[i], y_peer)

    def copy_a2(i):
        return send(o2.at[i, 0], i2.at[i, 0], sa2.at[i], ra2.at[i], y_peer)

    def copy_b2(i):
        return send(o2.at[i, 1], i2.at[i, 1], sb2.at[i], rb2.at[i], x_peer)

    def z_peer(d):
        return lax.rem(z + d, depth) * 4 + plane

    def copy_z3(i):
        return send(o3.at[i], i3.at[i], sz3.at[i], rz3.at[i], z_peer(i + 1))

    def copy_zg(d):
        return send(slope_all.at[f], slope_all.at[f], szg.at[d], rzg.at[d], z_peer(d))

    def layer(d):
        return lax.rem(z - d + depth, depth) * 4

    def copy_xg(d):
        at = layer(d) + plane
        return send(slope_all.at[at], slope_all.at[at], sxg.at[d], rxg.at[d], x_peer)

    def copy_yg(d):
        at = layer(d) + plane
        return send(slope_all.at[at], slope_all.at[at], syg.at[d], ryg.at[d], y_peer)

    def copy_xd(d):
        at = layer(d) + (1 - y) * 2 + x
        return send(slope_all.at[at, 0], slope_all.at[at, 0], sxd.at[d], rxd.at[d], x_peer)

    def copy_yd(d):
        at = layer(d) + y * 2 + 1 - x
        return send(slope_all.at[at, 1], slope_all.at[at, 1], syd.at[d], ryd.at[d], y_peer)

    def copy3(d):
        to = lax.rem(f + d, fields)
        return pltpu.make_async_remote_copy(
            out3.at[to], in3.at[f], s3.at[d], r3.at[d], device_id={"field": to}, device_id_type=MESH)

    def copyx(d):
        to = lax.rem(c + d, shards)
        return pltpu.make_async_remote_copy(
            wg_out.at[to], wg_in.at[c], sx.at[d], rx.at[d], device_id={"batch": to}, device_id_type=MESH)

    def each(first, last, copy, action):
        def step(d, carry):
            action(copy(d))
            return carry
        lax.fori_loop(first, last, step, 0)

    def wait_in(copy):
        copy.wait_recv()

    def wait_out(copy):
        copy.wait_send()

    def go(copy):
        copy.start()

    pl.semaphore_wait(barrier, fields - 1 + shards - 1)
    each(1, fields, copy1, go)

    w_copy.wait()
    w_slots = w_ref[...].astype(F32).reshape(fields - 1, half, part)
    gap = jnp.zeros((1, half, part), F32)
    w_block = lax.broadcasted_iota(jnp.int32, (fields, half, part), 0)
    w_wide = jnp.where(
        w_block < f,
        jnp.concatenate([w_slots, gap], 0),
        jnp.where(w_block > f, jnp.concatenate([gap, w_slots], 0), 0.0),
    )
    bias = jnp.broadcast_to(b_ref[...].astype(F32), (16, part))
    w_all[c] = jnp.concatenate([w_wide.reshape(pair_count, part), bias], 0).astype(BF16)
    each(1, shards, copyw, go)

    each(1, fields, copy1, wait_in)
    received = unfold_rows(in1[...].astype(F32), 2)
    rec_v[...] = received
    product = (mine_v[...] * received).reshape(pair_count, samples)
    pairs_t[...] = product.astype(BF16)
    pairs[...] = product.T.astype(BF16)
    each(1, shards, copyw, wait_in)

    weights = jnp.concatenate([w_all[s, :pair_count, :] for s in range(shards)], axis=1)

    def split_columns(t):
        return [fold_rows(t[:, :, p * (hid // 2):(p + 1) * (hid // 2)], fold) for p in range(2)]

    def pick(which, first, second):
        return jnp.where(which == 0, first, second)

    def stage1(i, carry):
        at = lax.rem(z + i + 1, depth) * (4 * rows)
        lhs = pairs[pl.ds(pl.multiple_of(at, 4 * rows), 4 * rows), :]
        t = jnp.dot(lhs, weights, preferred_element_type=F32).reshape(4, rows, hid)
        ta, tb = split_columns(t)
        ta = ta.reshape((2, 2) + ta.shape[1:])
        tb = tb.reshape((2, 2) + tb.shape[1:])
        keep1[i, 0] = pick(x, ta[:, 0], ta[:, 1])
        o1[i, 0] = pick(x, ta[:, 1], ta[:, 0]).astype(BF16)
        copy_a1(i).start()
        keep1[i, 1] = pick(y, tb[0], tb[1])
        o1[i, 1] = pick(y, tb[1], tb[0]).astype(BF16)
        copy_b1(i).start()
        return carry

    lax.fori_loop(0, depth, stage1, 0)

    def stage2(i, carry):
        copy_a1(i).wait_recv()
        ta = keep1[i, 0] + i1[i, 0].astype(F32)
        keep2[i, 0] = pick(y, ta[0], ta[1])
        o2[i, 0] = pick(y, ta[1], ta[0]).astype(BF16)
        copy_a2(i).start()
        copy_b1(i).wait_recv()
        tb = keep1[i, 1] + i1[i, 1].astype(F32)
        keep2[i, 1] = pick(x, tb[0], tb[1])
        o2[i, 1] = pick(x, tb[1], tb[0]).astype(BF16)
        copy_b2(i).start()
        return carry

    lax.fori_loop(0, depth, stage2, 0)

    def stage3(i, carry):
        copy_a2(i).wait_recv()
        copy_b2(i).wait_recv()
        o3[i] = (keep2[i] + i2[i].astype(F32)).astype(BF16)
        copy_z3(i).start()
        return carry

    lax.fori_loop(0, depth - 1, stage3, 0)
    copy_a2(depth - 1).wait_recv()
    copy_b2(depth - 1).wait_recv()
    acc[...] = keep2[depth - 1] + i2[depth - 1].astype(F32)

    def add(i, carry):
        copy_z3(i).wait_recv()
        acc[...] += i3[i].astype(F32)
        return carry

    lax.fori_loop(0, depth - 1, add, 0)
    g_copy.wait()
    bias_all = jnp.concatenate([w_all[s, pair_count:, :][:1].astype(F32) for s in range(shards)], axis=1)
    hidden = jnp.concatenate([unfold_rows(acc[p][None], fold)[0] for p in range(2)], axis=1) + bias_all
    gate = jax.nn.sigmoid(hidden)
    slope = g_blk[...].astype(F32) * gate * (1.0 + hidden * (1.0 - gate))
    slope_a, slope_b = split_columns(slope[None])
    slope_all[f] = jnp.concatenate([slope_a, slope_b], 0).astype(BF16)

    each(1, depth, copy_zg, go)
    copy_xg(0).start()
    copy_yg(0).start()

    def spread(d, carry):
        copy_zg(d).wait_recv()
        copy_xg(d).start()
        copy_yg(d).start()
        return carry

    lax.fori_loop(1, depth, spread, 0)

    def diagonal(d, carry):
        copy_yg(d).wait_recv()
        copy_xd(d).start()
        copy_xg(d).wait_recv()
        copy_yd(d).start()
        return carry

    lax.fori_loop(0, depth, diagonal, 0)
    each(0, depth, copy_xd, wait_in)
    each(0, depth, copy_yd, wait_in)

    if fold == 1:
        halves = [slope_all[:, p].reshape(samples, hid // 2) for p in range(2)]
    else:
        halves = [
            unfold_rows(slope_all[:, p].astype(F32), fold).reshape(samples, hid // 2).astype(BF16)
            for p in range(2)
        ]
    slope_full = jnp.concatenate(halves, axis=1)
    grad_t = lax.dot_general(weights, slope_full, (((1,), (1,)), ((), ())), preferred_element_type=F32)
    grad_t = grad_t.reshape(fields, half, samples)
    out3[...] = fold_rows(grad_t * mine_v[...], 2).astype(BF16)
    each(1, fields, copy3, go)
    rec_v[...] = grad_t * rec_v[...]

    term = jnp.dot(pairs_t[...], slope_full, preferred_element_type=F32)
    for s in range(shards):
        wg_acc[s] = term[:, s * part:(s + 1) * part]
    wg_out[...] = wg_acc[...].astype(BF16)
    each(1, shards, copyx, go)

    scale = 1.0 / jnp.sqrt(cnt_ref[...].astype(F32))
    each(1, fields, copy3, wait_in)
    back = unfold_rows(in3[...].astype(F32), 2) * scale[None]
    local = rec_v[...] * scale[None]
    full = jnp.concatenate([jnp.where(below, back, local), jnp.where(below, local, back)], axis=1)
    eg_ref[...] = full.reshape(fields * 2 * half, samples).T.astype(BF16)

    each(1, shards, copyx, wait_in)
    total = wg_acc[c]
    for d in range(1, shards):
        total = total + wg_in[lax.rem(c + d, shards)].astype(F32)
    wg3 = total.reshape(fields, half, part)
    slot = lax.broadcasted_iota(jnp.int32, (fields - 1, half, part), 0)
    wg_ref[...] = jnp.where(slot < f, wg3[:-1], wg3[1:]).reshape(pair_count - half, part)

    for first, last, copy in (
            (1, fields, copy1), (1, shards, copyw), (0, depth, copy_a1), (0, depth, copy_b1),
            (0, depth, copy_a2), (0, depth, copy_b2), (0, depth - 1, copy_z3), (1, depth, copy_zg),
            (0, depth, copy_xg), (0, depth, copy_yg), (0, depth, copy_xd), (0, depth, copy_yd),
            (1, fields, copy3), (1, shards, copyx)):
        each(first, last, copy, wait_out)


def body(pooled, counts, w_pairs, bias_terms, grad_act):
    fields = lax.axis_size("field")
    shards = lax.axis_size("batch")
    samples = pooled.shape[0]
    width = pooled.shape[2]
    part = w_pairs.shape[2]
    hid = grad_act.shape[1]
    half = width // fields // 2
    rows = samples // fields
    fold = max(1, 16 // rows)
    pair_count = fields * half
    packed = (fields, 2 * half, samples // 2)
    block = (rows * fold, hid // 2 // fold)
    depth = fields // 4
    vmem = pl.BlockSpec(memory_space=pltpu.VMEM)
    anywhere = pl.BlockSpec(memory_space=pl.ANY)
    dma = pltpu.SemaphoreType.DMA
    entry, weight = pl.pallas_call(
        functools.partial(kernel, fields, shards, fold),
        out_shape=(
            jax.ShapeDtypeStruct((samples, width), BF16),
            jax.ShapeDtypeStruct((pair_count - half, part), F32),
        ),
        in_specs=[anywhere, vmem, anywhere, vmem, anywhere],
        out_specs=(vmem, vmem),
        scratch_shapes=[
            pltpu.VMEM((samples, width), BF16),
            pltpu.VMEM((pair_count - half, part), BF16),
            pltpu.VMEM(packed, BF16),
            pltpu.VMEM(packed, BF16),
            pltpu.VMEM((fields, half, samples), F32),
            pltpu.VMEM((fields, half, samples), F32),
            pltpu.VMEM((shards, pair_count + 16, part), BF16),
            pltpu.VMEM((pair_count, samples), BF16),
            pltpu.VMEM((samples, pair_count), BF16),
            pltpu.VMEM((rows, hid), BF16),
            pltpu.VMEM((depth, 2, 2) + block, F32),
            pltpu.VMEM((depth, 2, 2) + block, BF16),
            pltpu.VMEM((depth, 2, 2) + block, BF16),
            pltpu.VMEM((depth, 2) + block, F32),
            pltpu.VMEM((depth, 2) + block, BF16),
            pltpu.VMEM((depth, 2) + block, BF16),
            pltpu.VMEM((depth, 2) + block, BF16),
            pltpu.VMEM((depth, 2) + block, BF16),
            pltpu.VMEM((2,) + block, F32),
            pltpu.VMEM((fields, 2) + block, BF16),
            pltpu.VMEM(packed, BF16),
            pltpu.VMEM(packed, BF16),
            pltpu.VMEM((shards, pair_count, part), BF16),
            pltpu.VMEM((shards, pair_count, part), BF16),
            pltpu.VMEM((shards, pair_count, part), F32),
            dma((fields,)), dma((fields,)), dma((shards,)), dma((shards,)),
            dma((fields,)), dma((fields,)), dma((shards,)), dma((shards,)),
        ] + [dma((depth,))] * 20 + [dma((3,))],
        compiler_params=pltpu.CompilerParams(
            collective_id=0, has_side_effects=True, vmem_limit_bytes=48 * 1024 * 1024),
    )(
        pooled.reshape(samples, width),
        counts.reshape(1, samples),
        w_pairs[0],
        bias_terms.reshape(1, part),
        grad_act.reshape(fields, rows, hid),
    )
    return entry.reshape(samples, 1, width), weight[None]


def solution(mesh):
    in_specs = (
        P("batch", "field", None),
        P("batch", "field"),
        P("field", None, "batch"),
        P("batch"),
        P("batch", None),
    )
    out_specs = (P("batch", "field", None), P("field", None, "batch"))
    return jax.shard_map(body, mesh=mesh, in_specs=in_specs, out_specs=out_specs, check_vma=False)
```

time: 73.9 us -> 54.8 us (0.74)
  Pallas kernels: 67.8 us -> 48.8 us
    pallas_call x1, Pallas kernels: 67.8 us -> 48.8 us  [body(): pl.pallas_call(functools.partial(kernel, fields, shards, fold), out_shape...]
where the time goes in v2:
time: 54.8 us; the launch traced here: 54.6 us
  Pallas kernels  48.8 us (89%)
  local copies, waits for them, and re-layouts  5.15 us (9%)
  between operations  0.66 us (1%)
    pallas_call x1, Pallas kernels, body(): pl.pallas_call(functools.partial(kernel, fields, shards, fold), out_shape...  48.8 us
    unnamed x12, local copies, waits for them, and re-layouts  5.15 us

profile of v2, /device:TPU:0, one launch (start us, length us, event | category | flops | bytes accessed | tf_op | source)
XLA Modules:
  0.0 54.6 jit_solution(1380453661454352400)
XLA Ops:
  0.6 0.0 copy-start.4
  0.6 0.0 copy-start.3
  0.6 0.7 %copy-done.4 = bf16[512]{0:T(512)(128)(2,1)S(1)} copy-done((bf16[512]{0:T(512)(128)(2,1)S(1)}, bf16[512]{0:T(512)(128)(2,1)}, u32[]{:S(2)}) %copy-start.4) | copy-done | bytes 1048
  1.3 0.0 copy-done.3
  1.3 0.0 copy-start
  1.3 1.2 %copy-done = bf16[512,1024]{1,0:T(8,128)(2,1)S(1)} copy-done((bf16[512,1024]{1,0:T(8,128)(2,1)S(1)}, bf16[512,1024]{1,0:T(8,128)(2,1)}, u32[]{:S(2)}) %copy-start) | copy-done | bytes 1048600
  2.6 0.0 copy-start.1
  2.6 0.9 %copy-done.1 = bf16[512,1,256]{2,0,1:T(8,128)(2,1)S(1)} copy-done((bf16[512,1,256]{2,0,1:T(8,128)(2,1)S(1)}, bf16[512,1,256]{2,0,1:T(8,128)(2,1)}, u32[]{:S(2)}) %copy-start.1) | copy-done | bytes 262168
  3.5 0.0 copy-start.2
  3.5 0.9 %copy-done.2 = bf16[1,120,512]{2,1,0:T(8,128)(2,1)S(1)} copy-done((bf16[1,120,512]{2,1,0:T(8,128)(2,1)S(1)}, bf16[1,120,512]{2,1,0:T(8,128)(2,1)}, u32[]{:S(2)}) %copy-start.2) | copy-done | bytes 122904
  4.4 48.8 %shard_map.68 = (bf16[512,256]{1,0:T(8,128)(2,1)S(1)}, f32[120,512]{1,0:T(8,128)S(1)}) custom-call(bf16[512,256]{1,0:T(8,128)(2,1)S(1)} %bitcast.8, s32[1,512]{1,0:T(1,128)S(1)} %bitcast.11, bf16[120,512]{1,0:T(8,128)(2,1)S(1)} %bitcast.10, bf16[1,512]{1,0:T(2,128)(2,1)S(1)} %reshape.21.b_ref, bf16[16,32,1024]{2,1,0:T(8,128)(2,1)S(1)} %bitcast.6), custom_call_target="tpu_custom_call" | custom-call | tf_op jit(solution)/shard_map/pallas_call | solution.py:335
  53.2 0.7 %copy.9 = bf16[512,1,256]{2,0,1:T(8,128)(2,1)} copy(bf16[512,1,256]{2,0,1:T(8,128)(2,1)S(1)} %bitcast.7) | data formatting | bytes 524288
  53.9 0.7 %copy.10 = f32[1,120,512]{2,1,0:T(8,128)} copy(f32[1,120,512]{2,1,0:T(8,128)S(1)} %bitcast.9) | data formatting | bytes 491520
  (1 shorter events, 0.0 us)
Async XLA Ops:
  0.6 0.7 %copy-start.4 = (bf16[512]{0:T(512)(128)(2,1)S(1)}, bf16[512]{0:T(512)(128)(2,1)}, u32[]{:S(2)}) copy-start(bf16[512]{0:T(512)(128)(2,1)} %param.8) | copy-start | bytes 3076
  0.6 0.7 %copy-start.3 = (s32[512,1]{0,1:T(1,128)S(1)}, s32[512,1]{0,1:T(1,128)}, u32[]{:S(2)}) copy-start(s32[512,1]{0,1:T(1,128)} %param.6) | copy-start | bytes 6148
  1.3 1.2 %copy-start = (bf16[512,1024]{1,0:T(8,128)(2,1)S(1)}, bf16[512,1024]{1,0:T(8,128)(2,1)}, u32[]{:S(2)}) copy-start(bf16[512,1024]{1,0:T(8,128)(2,1)} %param.9) | copy-start | bytes 3145732
  2.6 0.9 %copy-start.1 = (bf16[512,1,256]{2,0,1:T(8,128)(2,1)S(1)}, bf16[512,1,256]{2,0,1:T(8,128)(2,1)}, u32[]{:S(2)}) copy-start(bf16[512,1,256]{2,0,1:T(8,128)(2,1)} %param.5) | copy-start | bytes 786436
  3.5 0.9 %copy-start.2 = (bf16[1,120,512]{2,1,0:T(8,128)(2,1)S(1)}, bf16[1,120,512]{2,1,0:T(8,128)(2,1)}, u32[]{:S(2)}) copy-start(bf16[1,120,512]{2,1,0:T(8,128)(2,1)} %param.7) | copy-start | bytes 368644

commit v3 on v2

v3 whole, which is shorter than its diff:
```python
import functools

import jax
import jax.numpy as jnp
from jax import lax
from jax.experimental import pallas as pl
from jax.experimental.pallas import tpu as pltpu
from jax.sharding import PartitionSpec as P

MESH = pl.DeviceIdType.MESH
F32 = jnp.float32
BF16 = jnp.bfloat16


def fold_rows(x, parts):
    if parts == 1:
        return x
    width = x.shape[2] // parts
    return jnp.concatenate([x[:, :, p * width:(p + 1) * width] for p in range(parts)], axis=1)


def unfold_rows(x, parts):
    if parts == 1:
        return x
    height = x.shape[1] // parts
    return jnp.concatenate([x[:, p * height:(p + 1) * height, :] for p in range(parts)], axis=2)


def kernel(fields, shards, fold, phases, e_hbm, cnt_ref, w_hbm, b_ref, g_hbm, eg_ref, wg_ref,
           e_ref, w_ref, out1, in1, mine_v, rec_v, w_all, pairs_t, pairs, g_blk,
           keep1, o1, i1, keep2, o2, i2, o3, i3, acc,
           slope_all, out3, in3, wg_out, wg_in, wg_acc, wg_full, grad_acc,
           s1, r1, sw, rw, s3, r3, sx, rx,
           sa1, ra1, sb1, rb1, sa2, ra2, sb2, rb2, sz3, rz3,
           szg, rzg, sxg, rxg, syg, ryg, sxd, rxd, syd, ryd, sl):
    f = lax.axis_index("field")
    c = lax.axis_index("batch")
    samples = e_ref.shape[0]
    hid = g_hbm.shape[2]
    rows = samples // fields
    part = w_ref.shape[1]
    half = 8
    pair_count = fields * half
    depth = fields // 4
    x = lax.rem(f, 2)
    y = lax.rem(f // 2, 2)
    z = f // 4
    plane = lax.rem(f, 4)
    x_peer = f + 1 - 2 * x
    y_peer = f + 2 - 4 * y

    e_copy = pltpu.make_async_copy(e_hbm, e_ref, sl.at[0])
    w_copy = pltpu.make_async_copy(w_hbm, w_ref, sl.at[1])
    g_copy = pltpu.make_async_copy(g_hbm.at[f], g_blk, sl.at[2])
    e_copy.start()
    w_copy.start()
    g_copy.start()

    barrier = pltpu.get_barrier_semaphore()

    def greet(d, carry):
        pl.semaphore_signal(barrier, inc=1, device_id={"field": lax.rem(f + d, fields)}, device_id_type=MESH)
        return carry

    def greet_batch(d, carry):
        pl.semaphore_signal(barrier, inc=1, device_id={"batch": lax.rem(c + d, shards)}, device_id_type=MESH)
        return carry

    lax.fori_loop(1, fields, greet, 0)
    lax.fori_loop(1, shards, greet_batch, 0)

    e_copy.wait()
    e_t = e_ref[...].astype(F32).T.reshape(fields, 2 * half, samples)
    block = lax.broadcasted_iota(jnp.int32, (fields, half, samples), 0)
    below = block < f
    low, high = e_t[:, :half, :], e_t[:, half:, :]
    mine_v[...] = jnp.where(below, high, low)
    out1[...] = fold_rows(jnp.where(below, low, high), 2).astype(BF16)
    blank = jnp.zeros((1,) + in1.shape[1:], BF16)
    in1[pl.ds(f, 1)] = blank
    in3[pl.ds(f, 1)] = blank

    def copy1(d):
        to = lax.rem(f + d, fields)
        return pltpu.make_async_remote_copy(
            out1.at[to], in1.at[f], s1.at[d], r1.at[d], device_id={"field": to}, device_id_type=MESH)

    def copyw(d):
        return pltpu.make_async_remote_copy(
            w_all.at[c], w_all.at[c], sw.at[d], rw.at[d],
            device_id={"batch": lax.rem(c + d, shards)}, device_id_type=MESH)

    def send(src, dst, s, r, to):
        return pltpu.make_async_remote_copy(
            src, dst, s, r, device_id={"field": to}, device_id_type=MESH)

    def copy_a1(p, i):
        return send(o1.at[p, i, 0], i1.at[p, i, 0], sa1.at[p, i], ra1.at[p, i], x_peer)

    def copy_b1(p, i):
        return send(o1.at[p, i, 1], i1.at[p, i, 1], sb1.at[p, i], rb1.at[p, i], y_peer)

    def copy_a2(p, i):
        return send(o2.at[p, i, 0], i2.at[p, i, 0], sa2.at[p, i], ra2.at[p, i], y_peer)

    def copy_b2(p, i):
        return send(o2.at[p, i, 1], i2.at[p, i, 1], sb2.at[p, i], rb2.at[p, i], x_peer)

    def z_peer(d):
        return lax.rem(z + d, depth) * 4 + plane

    def copy_z3(p, i):
        return send(o3.at[p, i], i3.at[p, i], sz3.at[p, i], rz3.at[p, i], z_peer(i + 1))

    def copy_zg(p, d):
        return send(slope_all.at[f, p], slope_all.at[f, p], szg.at[p, d], rzg.at[p, d], z_peer(d))

    def layer(d):
        return lax.rem(z - d + depth, depth) * 4

    def copy_xg(p, d):
        at = layer(d) + plane
        return send(slope_all.at[at, p], slope_all.at[at, p], sxg.at[p, d], rxg.at[p, d], x_peer)

    def copy_yg(p, d):
        at = layer(d) + plane
        return send(slope_all.at[at, p], slope_all.at[at, p], syg.at[p, d], ryg.at[p, d], y_peer)

    def copy_xd(p, d):
        at = layer(d) + (1 - y) * 2 + x
        return send(slope_all.at[at, p, 0], slope_all.at[at, p, 0], sxd.at[p, d], rxd.at[p, d], x_peer)

    def copy_yd(p, d):
        at = layer(d) + y * 2 + 1 - x
        return send(slope_all.at[at, p, 1], slope_all.at[at, p, 1], syd.at[p, d], ryd.at[p, d], y_peer)

    def copy3(d):
        to = lax.rem(f + d, fields)
        return pltpu.make_async_remote_copy(
            out3.at[to], in3.at[f], s3.at[d], r3.at[d], device_id={"field": to}, device_id_type=MESH)

    def copyx(d):
        to = lax.rem(c + d, shards)
        return pltpu.make_async_remote_copy(
            wg_out.at[to], wg_in.at[c], sx.at[d], rx.at[d], device_id={"batch": to}, device_id_type=MESH)

    def each(first, last, copy, action):
        def step(d, carry):
            action(copy(d))
            return carry
        lax.fori_loop(first, last, step, 0)

    def wait_in(copy):
        copy.wait_recv()

    def wait_out(copy):
        copy.wait_send()

    def go(copy):
        copy.start()

    pl.semaphore_wait(barrier, fields - 1 + shards - 1)
    each(1, fields, copy1, go)

    w_copy.wait()
    w_slots = w_ref[...].astype(F32).reshape(fields - 1, half, part)
    gap = jnp.zeros((1, half, part), F32)
    w_block = lax.broadcasted_iota(jnp.int32, (fields, half, part), 0)
    w_wide = jnp.where(
        w_block < f,
        jnp.concatenate([w_slots, gap], 0),
        jnp.where(w_block > f, jnp.concatenate([gap, w_slots], 0), 0.0),
    )
    bias = jnp.broadcast_to(b_ref[...].astype(F32), (16, part))
    w_all[c] = jnp.concatenate([w_wide.reshape(pair_count, part), bias], 0).astype(BF16)
    each(1, shards, copyw, go)

    each(1, fields, copy1, wait_in)
    received = unfold_rows(in1[...].astype(F32), 2)
    rec_v[...] = received
    product = (mine_v[...] * received).reshape(pair_count, samples)
    pairs_t[...] = product.astype(BF16)
    pairs[...] = product.T.astype(BF16)
    each(1, shards, copyw, wait_in)

    weights = jnp.concatenate([w_all[s, :pair_count, :] for s in range(shards)], axis=1)

    wide = hid // phases

    def split_columns(t):
        return [fold_rows(t[:, :, p * (wide // 2):(p + 1) * (wide // 2)], fold) for p in range(2)]

    def pick(which, first, second):
        return jnp.where(which == 0, first, second)

    def stage1(p):
        def step(i, carry):
            at = lax.rem(z + i + 1, depth) * (4 * rows)
            lhs = pairs[pl.ds(pl.multiple_of(at, 4 * rows), 4 * rows), :]
            t = jnp.dot(lhs, weights[:, p * wide:(p + 1) * wide], preferred_element_type=F32)
            ta, tb = split_columns(t.reshape(4, rows, wide))
            ta = ta.reshape((2, 2) + ta.shape[1:])
            tb = tb.reshape((2, 2) + tb.shape[1:])
            o1[p, i, 0] = pick(x, ta[:, 1], ta[:, 0]).astype(BF16)
            copy_a1(p, i).start()
            o1[p, i, 1] = pick(y, tb[1], tb[0]).astype(BF16)
            copy_b1(p, i).start()
            keep1[p, i, 0] = pick(x, ta[:, 0], ta[:, 1])
            keep1[p, i, 1] = pick(y, tb[0], tb[1])
            return carry

        lax.fori_loop(0, depth, step, 0)

    def stage2(p):
        def step(i, carry):
            copy_a1(p, i).wait_recv()
            ta = keep1[p, i, 0] + i1[p, i, 0].astype(F32)
            o2[p, i, 0] = pick(y, ta[1], ta[0]).astype(BF16)
            copy_a2(p, i).start()
            keep2[p, i, 0] = pick(y, ta[0], ta[1])
            copy_b1(p, i).wait_recv()
            tb = keep1[p, i, 1] + i1[p, i, 1].astype(F32)
            o2[p, i, 1] = pick(x, tb[1], tb[0]).astype(BF16)
            copy_b2(p, i).start()
            keep2[p, i, 1] = pick(x, tb[0], tb[1])
            return carry

        lax.fori_loop(0, depth, step, 0)

    def stage3(p):
        def step(i, carry):
            copy_a2(p, i).wait_recv()
            copy_b2(p, i).wait_recv()
            o3[p, i] = (keep2[p, i] + i2[p, i].astype(F32)).astype(BF16)
            copy_z3(p, i).start()
            return carry

        lax.fori_loop(0, depth - 1, step, 0)
        copy_a2(p, depth - 1).wait_recv()
        copy_b2(p, depth - 1).wait_recv()
        acc[p] = keep2[p, depth - 1] + i2[p, depth - 1].astype(F32)

    bias_all = jnp.concatenate([w_all[s, pair_count:, :][:1].astype(F32) for s in range(shards)], axis=1)

    def activate(p):
        def add(i, carry):
            copy_z3(p, i).wait_recv()
            acc[p] += i3[p, i].astype(F32)
            return carry

        lax.fori_loop(0, depth - 1, add, 0)
        columns = slice(p * wide, (p + 1) * wide)
        hidden = jnp.concatenate([unfold_rows(acc[p, u][None], fold)[0] for u in range(2)], axis=1)
        hidden = hidden + bias_all[:, columns]
        gate = jax.nn.sigmoid(hidden)
        slope = g_blk[:, columns].astype(F32) * gate * (1.0 + hidden * (1.0 - gate))
        slope_a, slope_b = split_columns(slope[None])
        slope_all[f, p] = jnp.concatenate([slope_a, slope_b], 0).astype(BF16)
        each(1, depth, functools.partial(copy_zg, p), go)
        copy_xg(p, 0).start()
        copy_yg(p, 0).start()

    def spread(p):
        def step(d, carry):
            copy_zg(p, d).wait_recv()
            copy_xg(p, d).start()
            copy_yg(p, d).start()
            return carry

        lax.fori_loop(1, depth, step, 0)

    def diagonal(p):
        def step(d, carry):
            copy_yg(p, d).wait_recv()
            copy_xd(p, d).start()
            copy_xg(p, d).wait_recv()
            copy_yd(p, d).start()
            return carry

        lax.fori_loop(0, depth, step, 0)

    def gathered(p):
        each(0, depth, functools.partial(copy_xd, p), wait_in)
        each(0, depth, functools.partial(copy_yd, p), wait_in)
        if fold == 1:
            halves = [slope_all[:, p, u].reshape(samples, wide // 2) for u in range(2)]
        else:
            halves = [
                unfold_rows(slope_all[:, p, u].astype(F32), fold).reshape(samples, wide // 2).astype(BF16)
                for u in range(2)
            ]
        return jnp.concatenate(halves, axis=1)

    def grad_part(p, slope):
        return lax.dot_general(
            weights[:, p * wide:(p + 1) * wide], slope, (((1,), (1,)), ((), ())), preferred_element_type=F32)

    def weight_part(p, slope):
        wg_full[:, p * wide:(p + 1) * wide] = jnp.dot(pairs_t[...], slope, preferred_element_type=F32)

    for stage in (stage1, stage2, stage3):
        for p in range(phases):
            stage(p)
    g_copy.wait()
    for stage in (activate, spread, diagonal):
        for p in range(phases):
            stage(p)

    for p in range(phases):
        slope = gathered(p)
        if p == 0:
            grad_acc[...] = grad_part(p, slope)
        elif p < phases - 1:
            grad_acc[...] += grad_part(p, slope)
        if p < phases - 1:
            weight_part(p, slope)
    grad_t = (grad_acc[...] + grad_part(phases - 1, slope)).reshape(fields, half, samples)
    out3[...] = fold_rows(grad_t * mine_v[...], 2).astype(BF16)
    each(1, fields, copy3, go)
    rec_v[...] = grad_t * rec_v[...]

    weight_part(phases - 1, slope)
    for s in range(shards):
        term = wg_full[:, s * part:(s + 1) * part]
        wg_acc[s] = term
        wg_out[s] = term.astype(BF16)
    each(1, shards, copyx, go)

    scale = 1.0 / jnp.sqrt(cnt_ref[...].astype(F32))
    each(1, fields, copy3, wait_in)
    back = unfold_rows(in3[...].astype(F32), 2) * scale[None]
    local = rec_v[...] * scale[None]
    full = jnp.concatenate([jnp.where(below, back, local), jnp.where(below, local, back)], axis=1)
    eg_ref[...] = full.reshape(fields * 2 * half, samples).T.astype(BF16)

    each(1, shards, copyx, wait_in)
    total = wg_acc[c]
    for d in range(1, shards):
        total = total + wg_in[lax.rem(c + d, shards)].astype(F32)
    wg3 = total.reshape(fields, half, part)
    slot = lax.broadcasted_iota(jnp.int32, (fields - 1, half, part), 0)
    wg_ref[...] = jnp.where(slot < f, wg3[:-1], wg3[1:]).reshape(pair_count - half, part)

    for first, last, copy in (
            (1, fields, copy1), (1, shards, copyw), (1, fields, copy3), (1, shards, copyx)):
        each(first, last, copy, wait_out)
    for p in range(phases):
        for first, last, copy in (
                (0, depth, copy_a1), (0, depth, copy_b1), (0, depth, copy_a2), (0, depth, copy_b2),
                (0, depth - 1, copy_z3), (1, depth, copy_zg), (0, depth, copy_xg), (0, depth, copy_yg),
                (0, depth, copy_xd), (0, depth, copy_yd)):
            each(first, last, functools.partial(copy, p), wait_out)


def body(pooled, counts, w_pairs, bias_terms, grad_act):
    fields = lax.axis_size("field")
    shards = lax.axis_size("batch")
    samples = pooled.shape[0]
    width = pooled.shape[2]
    part = w_pairs.shape[2]
    hid = grad_act.shape[1]
    half = width // fields // 2
    rows = samples // fields
    fold = max(1, 16 // rows)
    pair_count = fields * half
    packed = (fields, 2 * half, samples // 2)
    phases = 2
    block = (rows * fold, hid // phases // 2 // fold)
    depth = fields // 4
    vmem = pl.BlockSpec(memory_space=pltpu.VMEM)
    anywhere = pl.BlockSpec(memory_space=pl.ANY)
    dma = pltpu.SemaphoreType.DMA
    entry, weight = pl.pallas_call(
        functools.partial(kernel, fields, shards, fold, phases),
        out_shape=(
            jax.ShapeDtypeStruct((samples, width), BF16),
            jax.ShapeDtypeStruct((pair_count - half, part), F32),
        ),
        in_specs=[anywhere, vmem, anywhere, vmem, anywhere],
        out_specs=(vmem, vmem),
        scratch_shapes=[
            pltpu.VMEM((samples, width), BF16),
            pltpu.VMEM((pair_count - half, part), BF16),
            pltpu.VMEM(packed, BF16),
            pltpu.VMEM(packed, BF16),
            pltpu.VMEM((fields, half, samples), F32),
            pltpu.VMEM((fields, half, samples), F32),
            pltpu.VMEM((shards, pair_count + 16, part), BF16),
            pltpu.VMEM((pair_count, samples), BF16),
            pltpu.VMEM((samples, pair_count), BF16),
            pltpu.VMEM((rows, hid), BF16),
            pltpu.VMEM((phases, depth, 2, 2) + block, F32),
            pltpu.VMEM((phases, depth, 2, 2) + block, BF16),
            pltpu.VMEM((phases, depth, 2, 2) + block, BF16),
            pltpu.VMEM((phases, depth, 2) + block, F32),
            pltpu.VMEM((phases, depth, 2) + block, BF16),
            pltpu.VMEM((phases, depth, 2) + block, BF16),
            pltpu.VMEM((phases, depth, 2) + block, BF16),
            pltpu.VMEM((phases, depth, 2) + block, BF16),
            pltpu.VMEM((phases, 2) + block, F32),
            pltpu.VMEM((fields, phases, 2) + block, BF16),
            pltpu.VMEM(packed, BF16),
            pltpu.VMEM(packed, BF16),
            pltpu.VMEM((shards, pair_count, part), BF16),
            pltpu.VMEM((shards, pair_count, part), BF16),
            pltpu.VMEM((shards, pair_count, part), F32),
            pltpu.VMEM((pair_count, hid), F32),
            pltpu.VMEM((pair_count, samples), F32),
            dma((fields,)), dma((fields,)), dma((shards,)), dma((shards,)),
            dma((fields,)), dma((fields,)), dma((shards,)), dma((shards,)),
        ] + [dma((phases, depth))] * 20 + [dma((3,))],
        compiler_params=pltpu.CompilerParams(
            collective_id=0, has_side_effects=True, vmem_limit_bytes=48 * 1024 * 1024),
    )(
        pooled.reshape(samples, width),
        counts.reshape(1, samples),
        w_pairs[0],
        bias_terms.reshape(1, part),
        grad_act.reshape(fields, rows, hid),
    )
    return entry.reshape(samples, 1, width), weight[None]


def solution(mesh):
    in_specs = (
        P("batch", "field", None),
        P("batch", "field"),
        P("field", None, "batch"),
        P("batch"),
        P("batch", None),
    )
    out_specs = (P("batch", "field", None), P("field", None, "batch"))
    return jax.shard_map(body, mesh=mesh, in_specs=in_specs, out_specs=out_specs, check_vma=False)
```

time: 54.8 us -> 51.9 us (0.947)
  Pallas kernels: 48.8 us -> 45.8 us
    pallas_call x1, Pallas kernels: 48.8 us -> 45.8 us  [body(): pl.pallas_call(functools.partial(kernel, fields, shards, fold, phases), o...]
where the time goes in v3:
time: 51.9 us; the launch traced here: 51.7 us
  Pallas kernels  45.8 us (88%)
  local copies, waits for them, and re-layouts  5.15 us (10%)
  between operations  0.66 us (1%)
    pallas_call x1, Pallas kernels, body(): pl.pallas_call(functools.partial(kernel, fields, shards, fold, phases), o...  45.8 us
    unnamed x12, local copies, waits for them, and re-layouts  5.15 us

profile of v3, /device:TPU:0, one launch (start us, length us, event | category | flops | bytes accessed | tf_op | source)
XLA Modules:
  0.0 51.7 jit_solution(11591594704889605001)
XLA Ops:
  0.6 0.0 copy-start.4
  0.6 0.0 copy-start.3
  0.6 0.7 %copy-done.4 = bf16[512]{0:T(512)(128)(2,1)S(1)} copy-done((bf16[512]{0:T(512)(128)(2,1)S(1)}, bf16[512]{0:T(512)(128)(2,1)}, u32[]{:S(2)}) %copy-start.4) | copy-done | bytes 1048
  1.3 0.0 copy-done.3
  1.3 0.0 copy-start
  1.3 1.2 %copy-done = bf16[512,1024]{1,0:T(8,128)(2,1)S(1)} copy-done((bf16[512,1024]{1,0:T(8,128)(2,1)S(1)}, bf16[512,1024]{1,0:T(8,128)(2,1)}, u32[]{:S(2)}) %copy-start) | copy-done | bytes 1048600
  2.6 0.0 copy-start.1
  2.6 0.9 %copy-done.1 = bf16[512,1,256]{2,0,1:T(8,128)(2,1)S(1)} copy-done((bf16[512,1,256]{2,0,1:T(8,128)(2,1)S(1)}, bf16[512,1,256]{2,0,1:T(8,128)(2,1)}, u32[]{:S(2)}) %copy-start.1) | copy-done | bytes 262168
  3.5 0.0 copy-start.2
  3.5 0.9 %copy-done.2 = bf16[1,120,512]{2,1,0:T(8,128)(2,1)S(1)} copy-done((bf16[1,120,512]{2,1,0:T(8,128)(2,1)S(1)}, bf16[1,120,512]{2,1,0:T(8,128)(2,1)}, u32[]{:S(2)}) %copy-start.2) | copy-done | bytes 122904
  4.4 45.8 %shard_map.68 = (bf16[512,256]{1,0:T(8,128)(2,1)S(1)}, f32[120,512]{1,0:T(8,128)S(1)}) custom-call(bf16[512,256]{1,0:T(8,128)(2,1)S(1)} %bitcast.8, s32[1,512]{1,0:T(1,128)S(1)} %bitcast.11, bf16[120,512]{1,0:T(8,128)(2,1)S(1)} %bitcast.10, bf16[1,512]{1,0:T(2,128)(2,1)S(1)} %reshape.21.b_ref, bf16[16,32,1024]{2,1,0:T(8,128)(2,1)S(1)} %bitcast.6), custom_call_target="tpu_custom_call" | custom-call | tf_op jit(solution)/shard_map/pallas_call | solution.py:373
  50.3 0.7 %copy.9 = bf16[512,1,256]{2,0,1:T(8,128)(2,1)} copy(bf16[512,1,256]{2,0,1:T(8,128)(2,1)S(1)} %bitcast.7) | data formatting | bytes 524288
  51.0 0.7 %copy.10 = f32[1,120,512]{2,1,0:T(8,128)} copy(f32[1,120,512]{2,1,0:T(8,128)S(1)} %bitcast.9) | data formatting | bytes 491520
  (1 shorter events, 0.0 us)
Async XLA Ops:
  0.6 0.7 %copy-start.4 = (bf16[512]{0:T(512)(128)(2,1)S(1)}, bf16[512]{0:T(512)(128)(2,1)}, u32[]{:S(2)}) copy-start(bf16[512]{0:T(512)(128)(2,1)} %param.8) | copy-start | bytes 3076
  0.6 0.7 %copy-start.3 = (s32[512,1]{0,1:T(1,128)S(1)}, s32[512,1]{0,1:T(1,128)}, u32[]{:S(2)}) copy-start(s32[512,1]{0,1:T(1,128)} %param.6) | copy-start | bytes 6148
  1.3 1.2 %copy-start = (bf16[512,1024]{1,0:T(8,128)(2,1)S(1)}, bf16[512,1024]{1,0:T(8,128)(2,1)}, u32[]{:S(2)}) copy-start(bf16[512,1024]{1,0:T(8,128)(2,1)} %param.9) | copy-start | bytes 3145732
  2.6 0.9 %copy-start.1 = (bf16[512,1,256]{2,0,1:T(8,128)(2,1)S(1)}, bf16[512,1,256]{2,0,1:T(8,128)(2,1)}, u32[]{:S(2)}) copy-start(bf16[512,1,256]{2,0,1:T(8,128)(2,1)} %param.5) | copy-start | bytes 786436
  3.5 0.9 %copy-start.2 = (bf16[1,120,512]{2,1,0:T(8,128)(2,1)S(1)}, bf16[1,120,512]{2,1,0:T(8,128)(2,1)}, u32[]{:S(2)}) copy-start(bf16[1,120,512]{2,1,0:T(8,128)(2,1)} %param.7) | copy-start | bytes 368644

commit v4 on v3

--- a/solution.py
+++ b/solution.py
@@ -26,8 +26,8 @@
     return jnp.concatenate([x[:, p * height:(p + 1) * height, :] for p in range(parts)], axis=2)
 
 
-def kernel(fields, shards, fold, phases, e_hbm, cnt_ref, w_hbm, b_ref, g_hbm, eg_ref, wg_ref,
-           e_ref, w_ref, out1, in1, mine_v, rec_v, w_all, pairs_t, pairs, g_blk,
+def kernel(fields, shards, fold, phases, e_hbm, cnt_ref, w_hbm, b_ref, g_hbm, eg_hbm, wg_hbm,
+           e_ref, w_ref, eg_ref, wg_ref, out1, in1, mine_v, rec_v, w_all, pairs_t, pairs, g_blk,
            keep1, o1, i1, keep2, o2, i2, o3, i3, acc,
            slope_all, out3, in3, wg_out, wg_in, wg_acc, wg_full, grad_acc,
            s1, r1, sw, rw, s3, r3, sx, rx,
@@ -326,12 +326,13 @@
         wg_out[s] = term.astype(BF16)
     each(1, shards, copyx, go)
 
-    scale = 1.0 / jnp.sqrt(cnt_ref[...].astype(F32))
-    each(1, fields, copy3, wait_in)
-    back = unfold_rows(in3[...].astype(F32), 2) * scale[None]
-    local = rec_v[...] * scale[None]
-    full = jnp.concatenate([jnp.where(below, back, local), jnp.where(below, local, back)], axis=1)
-    eg_ref[...] = full.reshape(fields * 2 * half, samples).T.astype(BF16)
+    for first, last, copy in ((1, fields, copy1), (1, shards, copyw)):
+        each(first, last, copy, wait_out)
+    for p in range(phases):
+        for first, last, copy in (
+                (0, depth, copy_a1), (0, depth, copy_b1), (0, depth, copy_a2), (0, depth, copy_b2),
+                (0, depth - 1, copy_z3), (1, depth, copy_zg), (0, depth, copy_xg), (0, depth, copy_yg)):
+            each(first, last, functools.partial(copy, p), wait_out)
 
     each(1, shards, copyx, wait_in)
     total = wg_acc[c]
@@ -340,16 +341,31 @@
     wg3 = total.reshape(fields, half, part)
     slot = lax.broadcasted_iota(jnp.int32, (fields - 1, half, part), 0)
     wg_ref[...] = jnp.where(slot < f, wg3[:-1], wg3[1:]).reshape(pair_count - half, part)
-
-    for first, last, copy in (
-            (1, fields, copy1), (1, shards, copyw), (1, fields, copy3), (1, shards, copyx)):
-        each(first, last, copy, wait_out)
+    wg_write = pltpu.make_async_copy(wg_ref, wg_hbm, sl.at[1])
+    wg_write.start()
     for p in range(phases):
-        for first, last, copy in (
-                (0, depth, copy_a1), (0, depth, copy_b1), (0, depth, copy_a2), (0, depth, copy_b2),
-                (0, depth - 1, copy_z3), (1, depth, copy_zg), (0, depth, copy_xg), (0, depth, copy_yg),
-                (0, depth, copy_xd), (0, depth, copy_yd)):
-            each(first, last, functools.partial(copy, p), wait_out)
+        each(0, depth, functools.partial(copy_xd, p), wait_out)
+        each(0, depth, functools.partial(copy_yd, p), wait_out)
+
+    scale = 1.0 / jnp.sqrt(cnt_ref[...].astype(F32))
+    each(1, fields, copy3, wait_in)
+    back = unfold_rows(in3[...].astype(F32), 2) * scale[None]
+    local = rec_v[...] * scale[None]
+    full = jnp.concatenate([jnp.where(below, back, local), jnp.where(below, local, back)], axis=1)
+    full = full.reshape(fields * 2 * half, samples)
+    mid = samples // 2
+    eg_writes = []
+    for u in range(2):
+        span = pl.ds(u * mid, mid)
+        eg_ref[span, :] = full[:, u * mid:(u + 1) * mid].T.astype(BF16)
+        eg_writes.append(pltpu.make_async_copy(eg_ref.at[span], eg_hbm.at[span], sl.at[2 * u]))
+        eg_writes[-1].start()
+
+    each(1, fields, copy3, wait_out)
+    each(1, shards, copyx, wait_out)
+    wg_write.wait()
+    for write in eg_writes:
+        write.wait()
 
 
 def body(pooled, counts, w_pairs, bias_terms, grad_act):
@@ -368,7 +384,7 @@
     block = (rows * fold, hid // phases // 2 // fold)
     depth = fields // 4
     vmem = pl.BlockSpec(memory_space=pltpu.VMEM)
-    anywhere = pl.BlockSpec(memory_space=pl.ANY)
+    anywhere = pl.BlockSpec(memory_space=pltpu.HBM)
     dma = pltpu.SemaphoreType.DMA
     entry, weight = pl.pallas_call(
         functools.partial(kernel, fields, shards, fold, phases),
@@ -377,10 +393,12 @@
             jax.ShapeDtypeStruct((pair_count - half, part), F32),
         ),
         in_specs=[anywhere, vmem, anywhere, vmem, anywhere],
-        out_specs=(vmem, vmem),
+        out_specs=(anywhere, anywhere),
         scratch_shapes=[
             pltpu.VMEM((samples, width), BF16),
             pltpu.VMEM((pair_count - half, part), BF16),
+            pltpu.VMEM((samples, width), BF16),
+            pltpu.VMEM((pair_count - half, part), F32),
             pltpu.VMEM(packed, BF16),
             pltpu.VMEM(packed, BF16),
             pltpu.VMEM((fields, half, samples), F32),
@@ -410,7 +428,7 @@
             dma((fields,)), dma((fields,)), dma((shards,)), dma((shards,)),
         ] + [dma((phases, depth))] * 20 + [dma((3,))],
         compiler_params=pltpu.CompilerParams(
-            collective_id=0, has_side_effects=True, vmem_limit_bytes=48 * 1024 * 1024),
+            collective_id=0, has_side_effects=True, vmem_limit_bytes=60 * 1024 * 1024),
     )(
         pooled.reshape(samples, width),
         counts.reshape(1, samples),

time: 51.9 us -> 51.3 us (0.988)
  local copies, waits for them, and re-layouts: 5.15 us -> 3.66 us
  Pallas kernels: 45.8 us -> 46.8 us
    unnamed x12 -> x6, local copies, waits for them, and re-layouts: 5.15 us -> 3.08 us
    pallas_call x1, Pallas kernels: 45.8 us -> 46.8 us  [body(): pl.pallas_call(functools.partial(kernel, fields, shards, fold, phases), o...]
    reshape x1, local copies, waits for them, and re-layouts: 0.01 us -> 0.58 us  [body(): bias_terms.reshape(1, part)]
where the time goes in v4:
time: 51.3 us; the launch traced here: 51.1 us
  Pallas kernels  46.8 us (91%)
  local copies, waits for them, and re-layouts  3.66 us (7%)
  between operations  0.66 us (1%)
    pallas_call x1, Pallas kernels, body(): pl.pallas_call(functools.partial(kernel, fields, shards, fold, phases), o...  46.8 us
    unnamed x6, local copies, waits for them, and re-layouts  3.08 us

profile of v4, /device:TPU:0, one launch (start us, length us, event | category | flops | bytes accessed | tf_op | source)
XLA Modules:
  0.0 51.1 jit_solution(15317798816361695260)
XLA Ops:
  0.6 0.0 copy-start.1
  0.6 0.7 %copy-done.1 = bf16[512]{0:T(512)(128)(2,1)S(1)} copy-done((bf16[512]{0:T(512)(128)(2,1)S(1)}, bf16[512]{0:T(512)(128)(2,1)}, u32[]{:S(2)}) %copy-start.1) | copy-done | bytes 1048
  1.3 0.6 %reshape.21.b_ref = bf16[1,512]{1,0:T(2,128)(2,1)} reshape(bf16[512]{0:T(512)(128)(2,1)S(1)} %copy-done.1) | data formatting | bytes 2048 | tf_op jit(solution)/shard_map/reshape | solution.py:436
  1.9 46.8 %shard_map.68 = (bf16[512,256]{1,0:T(8,128)(2,1)}, f32[120,512]{1,0:T(8,128)}) custom-call(bf16[512,256]{1,0:T(8,128)(2,1)} %bitcast.8, s32[1,512]{1,0:T(1,128)} %bitcast.11, bf16[120,512]{1,0:T(8,128)(2,1)} %bitcast.10, bf16[1,512]{1,0:T(2,128)(2,1)} %reshape.21.b_ref, bf16[16,32,1024]{2,1,0:T(8,128)(2,1)} %bitcast.6), custom_call_target="tpu_custom_call" | custom-call | tf_op jit(solution)/shard_map/pallas_call | solution.py:389
  48.7 0.0 copy-start
  48.7 1.7 %copy.9 = bf16[512,1,256]{2,0,1:T(8,128)(2,1)} copy(bf16[512,1,256]{2,0,1:T(8,128)(2,1)} %bitcast.7) | data formatting | bytes 524288
  50.4 0.0 copy-done
  50.4 0.7 %copy.10 = f32[1,120,512]{2,1,0:T(8,128)} copy(f32[1,120,512]{2,1,0:T(8,128)S(1)} %bitcast.9) | data formatting | bytes 491520
Async XLA Ops:
  0.6 0.7 %copy-start.1 = (bf16[512]{0:T(512)(128)(2,1)S(1)}, bf16[512]{0:T(512)(128)(2,1)}, u32[]{:S(2)}) copy-start(bf16[512]{0:T(512)(128)(2,1)} %param.8) | copy-start | bytes 3076
  48.7 1.7 %copy-start = (f32[120,512]{1,0:T(8,128)S(1)}, f32[120,512]{1,0:T(8,128)}, u32[]{:S(2)}) copy-start(f32[120,512]{1,0:T(8,128)} %get-tuple-element.5) | copy-start | bytes 737284
